TPU v7x, 32 devices: a whole 2x2x4 slice. The times are simulated.
32 devices in a mesh: grp: 4 (over y, core), shard: 8 (over z, x).
Axes of the slice: x: 2, y: 2, z: 4, core: 2. Of those that a mesh axis runs over, the one named last changes fastest.
Arguments:
- layer_inner: float32 [4, 1600, 1600], P('grp', 'shard'), may hold values from -6 to 6
- layer_weights: float32 [1600, 1600], P('shard'), may hold values from -6 to 6
- layer_moment: float32 [1600, 1600], P('shard'), may hold values from -6 to 6
- embed_inner: float32 [4, 3200, 1600], P('grp', 'shard'), may hold values from -6 to 6
- embed_weights: float32 [3200, 1600], P(('shard', 'grp')), may hold values from -6 to 6
- embed_moment: float32 [3200, 1600], P(('shard', 'grp')), may hold values from -6 to 6
- basis: float32 [1600, 64], replicated, may hold values from -0.15625 to 0.15625
Outputs:
- layer_new: float32 [1600, 1600], P('shard')
- layer_moment_new: float32 [1600, 1600], P('shard')
- layer_copy: bfloat16 [1600, 1600], replicated
- embed_new: float32 [3200, 1600], P(('shard', 'grp'))
- embed_moment_new: float32 [3200, 1600], P(('shard', 'grp'))
All inputs are finite; a program needn't handle non-finite values.
Results may differ from a plain program's by a relative error of at most 0.0015.
Values may be sent and summed in bfloat16 or wider, within the bound.
A program may use at most 128 MiB of HBM per device.

v0:
```python
import jax
import jax.numpy as jnp
from jax import lax
from jax.sharding import PartitionSpec as P

outer_rate = 0.7
momentum_coef = 0.9


def nesterov(weights, moment, average):
    moment_new = momentum_coef * moment + average
    return (weights - outer_rate * (average + momentum_coef * moment_new), moment_new)


def per_device(
    layer_inner, layer_weights, layer_moment, embed_inner, embed_weights, embed_moment, basis
):
    groups = lax.axis_size("grp")
    inner_proj = jnp.dot(embed_inner[0], basis, precision=lax.Precision.HIGHEST)
    mean_proj = (
        lax.psum_scatter(
            inner_proj.astype(jnp.bfloat16), "grp", scatter_dimension=0, tiled=True
        ).astype(jnp.float32)
        / groups
    )
    factors = jnp.dot(embed_weights, basis, precision=lax.Precision.HIGHEST) - mean_proj
    embed_step = jnp.dot(factors, basis.T, precision=lax.Precision.HIGHEST)
    embed_new, embed_moment_new = nesterov(embed_weights, embed_moment, embed_step)
    own_diff = layer_weights - layer_inner[0]
    average = lax.psum(own_diff, "grp") / groups
    layer_new, layer_moment_new = nesterov(layer_weights, layer_moment, average)
    layer_copy = lax.all_gather(layer_new.astype(jnp.bfloat16), "shard", axis=0, tiled=True)
    return (layer_new, layer_moment_new, layer_copy, embed_new, embed_moment_new)


def solution(mesh):
    in_specs = (
        P("grp", "shard", None),
        P("shard", None),
        P("shard", None),
        P("grp", "shard", None),
        P(("shard", "grp"), None),
        P(("shard", "grp"), None),
        P(),
    )
    out_specs = (
        P("shard", None),
        P("shard", None),
        P(),
        P(("shard", "grp"), None),
        P(("shard", "grp"), None),
    )
    return jax.shard_map(
        per_device, mesh=mesh, in_specs=in_specs, out_specs=out_specs, check_vma=False
    )
```

profile of v0, /device:TPU:0, one launch (start us, length us, event | category | flops | bytes accessed | tf_op | source)
XLA Modules:
  0.0 156.8 jit_solution(17572636539259694825)
XLA Ops:
  7.2 0.0 copy-start
  7.2 0.0 all-reduce.4.cloned.1.call-start
  7.2 3.1 %bitcast_subtract_fusion = f32[200,1600]{1,0:T(8,128)} fusion(f32[200,1600]{1,0:T(8,128)} %param.8, f32[1,200,1600]{2,1,0:T(8,128)} %param.7), kind=kLoop, calls=%fused_computation.2 | loop fusion | flops 320000 | bytes 3840000 | tf_op jit(solution)/shard_map/sub | solution.py:29
  10.3 0.0 all-reduce.4.cloned.1.call-update
  10.3 0.0 copy-start.1
  10.3 0.0 all-gather.2.cloned.1.call-start
  10.4 42.7 %all-reduce.4.cloned.1.call-done = f32[200,1600]{1,0:T(8,128)} async-done(((f32[200,1600]{1,0:T(8,128)}), f32[200,1600]{1,0:T(8,128)}) %all-reduce.4.cloned.1.call-update) | async-done | bytes 1280016 | tf_op jit(solution)/shard_map/psum | solution.py:30
  53.0 4.2 %fusion.14 = (bf16[200,1600]{1,0:T(8,128)(2,1)}, f32[200,1600]{1,0:T(8,128)}, f32[200,1600]{1,0:T(8,128)}) fusion(f32[200,1600]{1,0:T(8,128)} %param.8, f32[200,1600]{1,0:T(8,128)} %all-reduce.4.cloned.1.call-done, f32[200,1600]{1,0:T(8,128)} %param.9), kind=kLoop, calls=%fused_computation.16 | loop fusion | flops 2560000 | bytes 7040000 | tf_op jit(solution)/shard_map/convert_element_type | solution.py:32
  57.2 0.0 all-gather.2.cloned.1.call-update
  57.3 0.0 copy-done
  57.3 0.0 copy-done.1
  57.3 0.0 copy-start.2
  57.3 2.2 %fusion.3 = bf16[400,64]{1,0:T(8,128)(2,1)S(1)} fusion(f32[1600,64]{0,1:T(8,128)S(1)} %copy-done.1, f32[1,400,1600]{2,1,0:T(8,128)S(1)} %copy-done), kind=kOutput, calls=%fused_computation.5 | convolution fusion | flops 491545600 | bytes 3020800 | tf_op jit(solution)/shard_map/dot_general | solution.py:19
  59.5 8.2 %fusion = bf16[112,64]{1,0:T(8,128)(2,1)S(1)} fusion(bf16[400,64]{1,0:T(8,128)(2,1)S(1)} %fusion.3), kind=kCustom, calls=%all-reduce-scatter | all-reduce-scatter fusion | flops 28673 | bytes 66048
  67.8 1.3 collective-permute-start
  69.1 1.8 %fusion.15 = f32[100,64]{1,0:T(8,128)S(1)} fusion(f32[100,1600]{1,0:T(8,128)} %param.11, f32[1600,64]{0,1:T(8,128)S(1)} %copy-done.1), kind=kOutput, calls=%fused_computation.17 | convolution fusion | flops 122880000 | bytes 1075200 | tf_op jit(solution)/shard_map/dot_general | solution.py:26
  70.9 0.0 copy-done.2
  70.9 0.6 dynamic-slice.4
  72.2 0.0 collective-permute-done
  72.2 0.3 concatenate
  72.5 3.2 %multiply_subtract_fusion.1 = (f32[100,1600]{1,0:T(8,128)}, f32[100,1600]{1,0:T(8,128)}) fusion(f32[100,1600]{1,0:T(8,128)} %param.11, f32[100,1600]{1,0:T(8,128)} %param.12, f32[1600,64]{0,1:T(8,128)S(1)} %copy-done.1, f32[100,64]{1,0:T(8,128)S(1)} %fusion.15, bf16[148,64]{1,0:T(8,128)(2,1)S(1)} %concatenate, u32[]{:S(6)} %subtract), kind=kOutput, calls=%fused_computation.6 | convolution fusion | flops 123859200 | bytes 3065860 | tf_op jit(solution)/shard_map/dot_general | solution.py:27
  75.7 69.0 %all-gather.2.cloned.1.call-done = bf16[1600,1600]{1,0:T(8,128)(2,1)} async-done(((bf16[200,1600]{1,0:T(8,128)(2,1)}), bf16[1600,1600]{1,0:T(8,128)(2,1)}) %all-gather.2.cloned.1.call-update) | async-done | bytes 5120016 | tf_op jit(solution)/shard_map/all_gather | solution.py:32
  144.7 5.3 %copy.14 = bf16[1600,1600]{1,0:T(8,128)(2,1)} copy(bf16[1600,1600]{1,0:T(8,128)(2,1)} %all-gather.2.cloned.1.call-done) | data formatting | bytes 10240000
  (1 shorter events, 0.0 us)
Async XLA Ops:
  7.2 50.1 %copy-start = (f32[1,400,1600]{2,1,0:T(8,128)S(1)}, f32[1,400,1600]{2,1,0:T(8,128)}, u32[]{:S(2)}) copy-start(f32[1,400,1600]{2,1,0:T(8,128)} %param.10) | copy-start | bytes 7680004
  7.2 45.9 %all-reduce.4.cloned.1.call-start = ((), (), s32[]{:S(2)}) async-start(), calls=%async_computation | async-start | bytes 2662400 | tf_op jit(solution)/shard_map/psum | solution.py:30
  10.3 47.0 %copy-start.1 = (f32[1600,64]{0,1:T(8,128)S(1)}, f32[1600,64]{0,1:T(8,128)}, u32[]{:S(2)}) copy-start(f32[1600,64]{0,1:T(8,128)} %param.13) | copy-start | bytes 1228804
  10.3 134.4 %all-gather.2.cloned.1.call-start = ((), (), s32[]{:S(2)}) async-start(), calls=%async_computation.1 | async-start | bytes 5990400 | tf_op jit(solution)/shard_map/all_gather | solution.py:32
  57.3 13.7 %copy-start.2 = (u32[32]{0:T(128)S(1)}, u32[32]{0:T(128)}, u32[]{:S(2)}) copy-start(u32[32]{0:T(128)} %constant.17) | copy-start | bytes 388
  67.8 4.4 %collective-permute-start = (bf16[36,64]{1,0:T(8,128)(2,1)S(1)}, bf16[36,64]{1,0:T(8,128)(2,1)S(1)}, u32[]{:S(2)}, u32[]{:S(2)}) collective-permute-start(bf16[36,64]{1,0:T(8,128)(2,1)S(1)} %slice), channel_id=1, source_target_pairs={{0,8},{8,16},{16,24},{1,9},{9,17},{17,25},{2,10},{10,18},{18,26},{... | collective-permute-start | bytes 13832
Sparse Core Ops, SparseCore 0:
  11.0 42.0 all-reduce.3
  57.4 87.2 all-gather.1
where the time goes:
time: 157 us
  waiting for transfers between devices  112 us (71%)
  between operations  14.8 us (9%)
  blocking collectives  8.23 us (5%)
  other arithmetic  7.27 us (5%)
  matrix products  7.27 us (5%)
  local copies, waits for them, and re-layouts  6.17 us (4%)
    all_gather x1, waiting for transfers between devices, per_device(): lax.all_gather(layer_new.astype(jnp.bfloat16), 'shard', axis=0, tiled=True)  69 us
    psum x1, waiting for transfers between devices, per_device(): average = lax.psum(own_diff, 'grp') / groups  42.7 us
    unnamed x1, blocking collectives  8.23 us
    unnamed x10, local copies, waits for them, and re-layouts  6.17 us
    convert_element_type x1, other arithmetic, per_device(): layer_new.astype(jnp.bfloat16)  4.2 us
    dot_general x1, matrix products, per_device(): embed_step = jnp.dot(factors, basis.T, precision=lax.Precision.HIGHEST)  3.2 us
  transfers between devices with their start and end apart: 3, of which 2 were waited for; matrix products, arithmetic and copies ran while one was open for 10% of the time, Pallas kernels for 0%

commit v1 on v0

v1 whole, which is shorter than its diff:
```python
import functools

import jax
import jax.numpy as jnp
from jax import lax
from jax.experimental import pallas as pl
from jax.experimental.pallas import tpu as pltpu
from jax.sharding import PartitionSpec as P

outer_rate = 0.7
momentum_coef = 0.9
MESH = pl.DeviceIdType.MESH
LANES = 128
SLOPE = 13.0
SHIFT = 78.0


def nesterov(weights, moment, average):
    moment_new = momentum_coef * moment + average
    return (weights - outer_rate * (average + momentum_coef * moment_new), moment_new)


def encode(x):
    size = jnp.exp(jnp.abs(x) * SLOPE - SHIFT)
    return jnp.where(x < 0, -size, size).astype(jnp.bfloat16)


def decode(code):
    code = code.astype(jnp.float32)
    size = (jnp.log(jnp.abs(code)) + SHIFT) * (1.0 / SLOPE)
    return jnp.where(code < 0, -size, size)


def kernel(
    zs, groups, quarter,
    inner_h, w_h, m_h, einner_h, ew_h, em_h, bt_h,
    new_h, mom_h, all_h, enew_h, emom_h,
    inner, sib, w, m, einner, ew, em, bt, code, rcode, own, new, mom, proj, precv, enew, emom,
    in_sem, out_sem, a1_s, a1_r, a2_s, a2_r, a2f_s, a2f_r, e_s, e_r,
    up_s, dn_s, z_r, x_s, x_r, y_s, y_r, cz_s, cz_r, cx_s, cx_r, cy_s, cy_r,
):
    g, s = lax.axis_index("grp"), lax.axis_index("shard")
    y, c = g // 2, g % 2
    z, x = s // 2, s % 2
    width = inner_h.shape[-1]
    rows_e = ew_h.shape[0]
    tail0 = 4 * quarter
    tail_w = own.shape[-1] - tail0
    sib_id = (y * 2 + 1 - c, s)
    y_id = ((1 - y) * 2 + c, s)
    diag_id = ((1 - y) * 2 + 1 - c, s)
    x_id = (g, z * 2 + 1 - x)
    up_id = (g, s + 2)
    dn_id = (g, s - 2)
    has_up, has_dn = z < zs - 1, z > 0

    loads = [
        pltpu.make_async_copy(src, dst, in_sem.at[i])
        for i, (src, dst) in enumerate(
            [(inner_h.at[0], inner), (einner_h.at[0], einner), (bt_h, bt), (w_h, w), (m_h, m), (ew_h, ew), (em_h, em)]
        )
    ]
    for load in loads:
        load.start()

    barrier = pltpu.get_barrier_semaphore()
    for peer in (sib_id, y_id, diag_id, x_id):
        pl.semaphore_signal(barrier, inc=1, device_id=peer, device_id_type=MESH)

    @pl.when(has_up)
    def _():
        pl.semaphore_signal(barrier, inc=1, device_id=up_id, device_id_type=MESH)

    @pl.when(has_dn)
    def _():
        pl.semaphore_signal(barrier, inc=1, device_id=dn_id, device_id_type=MESH)

    pl.semaphore_wait(barrier, 4 + has_up.astype(jnp.int32) + has_dn.astype(jnp.int32))

    def remote(src, dst, ssem, rsem, peer):
        return pltpu.make_async_remote_copy(
            src_ref=src, dst_ref=dst, send_sem=ssem, recv_sem=rsem, device_id=peer, device_id_type=MESH
        )

    a1 = remote(inner_h.at[0], sib, a1_s, a1_r, sib_id)
    a1.start()
    loads[0].wait()
    a1.wait_recv()
    code[:, :tail0] = encode(inner[:, :tail0] + sib[:, :tail0])
    code[:, tail0:] = jnp.zeros_like(code[:, tail0:])
    code[:, tail0:width] = encode(inner[:, tail0:] + sib[:, tail0:])

    def cols(core, k):
        if k == 2:
            return pl.ds(tail0, tail_w)
        return pl.ds(pl.multiple_of((core * 2 + (y if k == 0 else 1 - y)) * quarter, LANES), quarter)

    def when_tail(core, k, f):
        if k == 2:
            pl.when(core == 1)(f)
        else:
            f()

    def a2(k):
        at = cols(c, 1 - k if k < 2 else 2)
        return remote(code.at[:, at], rcode.at[:, at], a2_s.at[k], a2_r.at[k], y_id)

    def a2_in(k):
        at = cols(c, k)
        return remote(code.at[:, at], rcode.at[:, at], a2_s.at[k], a2_r.at[k], y_id)

    def a2_fwd(core, k):
        at = cols(core, k)
        return remote(rcode.at[:, at], rcode.at[:, at], a2f_s.at[k], a2f_r.at[k], sib_id)

    for k in range(3):
        when_tail(c, k, lambda k=k: a2(k).start())

    loads[1].wait()
    loads[2].wait()
    nt = (((1,), (1,)), ((), ()))
    hi = lax.Precision.HIGHEST
    inner_proj = lax.dot_general(einner[...], bt[...], nt, precision=hi, preferred_element_type=jnp.float32)
    for i in range(groups):
        proj[i] = inner_proj[i * rows_e : (i + 1) * rows_e]
    e_peers = (sib_id, y_id, diag_id)

    def e_copy(i):
        return remote(proj.at[e_peers[i][0]], precv.at[i], e_s.at[i], e_r.at[i], e_peers[i])

    for i in range(3):
        e_copy(i).start()

    loads[3].wait()
    loads[4].wait()

    def update(at, at_io):
        total = decode(code[:, at_io]) + decode(rcode[:, at_io])
        average = w[:, at_io] - total * (1.0 / groups)
        new_v, mom_v = nesterov(w[:, at_io], m[:, at_io], average)
        new[:, at_io] = new_v
        mom[:, at_io] = mom_v
        own[:, at_io] = new_v.astype(jnp.bfloat16)

    def update_cols(core, k):
        if k == 2:
            update(None, pl.ds(tail0, width - tail0))
        else:
            update(None, cols(core, k))

    own[:, tail0:] = jnp.zeros_like(own[:, tail0:])

    def block(zsrc, xsrc, at):
        return all_h.at[zsrc * 2 + xsrc, :, at]

    def z_copy(zsrc, k, sems, peer, src=None):
        at = cols(c, k)
        dst = block(zsrc, x, at)
        return remote(dst if src is None else src.at[:, at], dst, sems.at[zsrc, k], z_r.at[zsrc, k], peer)

    def x_copy(zsrc, k, xsrc, src=None):
        at = cols(c, k)
        dst = block(zsrc, xsrc, at)
        return remote(dst if src is None else src.at[:, at], dst, x_s.at[zsrc, k // 2], x_r.at[zsrc, k // 2], x_id)

    def y_copy(zsrc, k):
        dst = block(zsrc, 1 - x, cols(c, k))
        return remote(dst, dst, y_s.at[zsrc], y_r.at[zsrc], y_id)

    def cz_copy(core, zsrc, k):
        dst = block(zsrc, x, cols(core, k))
        return remote(dst, dst, cz_s.at[zsrc, k], cz_r.at[zsrc, k], sib_id)

    def cx_copy(core, zsrc, k):
        dst = block(zsrc, 1 - x, cols(core, k))
        return remote(dst, dst, cx_s.at[zsrc, k // 2], cx_r.at[zsrc, k // 2], sib_id)

    def cy_copy(core, zsrc):
        dst = block(zsrc, 1 - x, cols(core, 1))
        return remote(dst, dst, cy_s.at[zsrc], cy_r.at[zsrc], sib_id)

    def own_piece(k):
        a2_in(k).wait_recv()
        a2_fwd(c, k).start()
        update_cols(c, k)

        @pl.when(has_up)
        def _():
            z_copy(z, k, up_s, up_id, own).start()

        @pl.when(has_dn)
        def _():
            z_copy(z, k, dn_s, dn_id, own).start()

        if k != 1:
            x_copy(z, k, x, own).start()

    for k in range(3):
        when_tail(c, k, lambda k=k: own_piece(k))

    def other_piece(k):
        a2_fwd(1 - c, k).wait_recv()
        update_cols(1 - c, k)

    for k in range(3):
        when_tail(1 - c, k, lambda k=k: other_piece(k))
    stores = [
        pltpu.make_async_copy(src, dst, out_sem.at[i])
        for i, (src, dst) in enumerate(
            [(own, all_h.at[s]), (new, new_h), (mom, mom_h), (enew, enew_h), (emom, emom_h)]
        )
    ]
    for store in stores[:3]:
        store.start()

    loads[5].wait()
    loads[6].wait()
    own_proj = lax.dot_general(ew[...], bt[...], nt, precision=hi, preferred_element_type=jnp.float32)
    for i in range(3):
        e_copy(i).wait_recv()
    mean_proj = (proj[g] + precv[0] + precv[1] + precv[2]) * (1.0 / groups)
    step = jnp.dot(own_proj - mean_proj, bt[...], precision=hi, preferred_element_type=jnp.float32)
    enew_v, emom_v = nesterov(ew[...], em[...], step)
    enew[...] = enew_v
    emom[...] = emom_v
    for store in stores[3:]:
        store.start()

    def z_arrive(zsrc, k, sems, peer, more):
        z_copy(zsrc, k, sems, peer).wait_recv()

        @pl.when(more)
        def _():
            z_copy(zsrc, k, sems, peer).start()

        if k != 1:
            x_copy(zsrc, k, x).start()
        cz_copy(c, zsrc, k).start()

    def x_arrive(zsrc, k):
        x_copy(zsrc, k, 1 - x).wait_recv()
        if k == 0:
            y_copy(zsrc, 0).start()
        cx_copy(c, zsrc, k).start()

    def y_arrive(zsrc):
        y_copy(zsrc, 1).wait_recv()
        cy_copy(c, zsrc).start()

    def both(d, f):
        @pl.when(z >= d)
        def _():
            f(z - d, up_s, up_id, has_up)

        @pl.when(z + d < zs)
        def _():
            f(z + d, dn_s, dn_id, has_dn)

    def x_all(zsrc):
        x_arrive(zsrc, 0)
        pl.when(c == 1)(lambda: x_arrive(zsrc, 2))

    def steps(d, carry):
        both(d, lambda zsrc, sems, peer, more: z_arrive(zsrc, 0, sems, peer, more))

        @pl.when(d == 1)
        def _():
            x_all(z)

        @pl.when(d == 2)
        def _():
            y_arrive(z)

        @pl.when(d > 1)
        def _():
            both(d - 1, lambda zsrc, sems, peer, more: x_all(zsrc))

        @pl.when(d > 2)
        def _():
            both(d - 2, lambda zsrc, sems, peer, more: y_arrive(zsrc))

        both(d, lambda zsrc, sems, peer, more: z_arrive(zsrc, 1, sems, peer, more))

        @pl.when(c == 1)
        def _():
            both(d, lambda zsrc, sems, peer, more: z_arrive(zsrc, 2, sems, peer, more))

        return carry

    lax.fori_loop(1, zs, steps, 0)
    both(zs - 1, lambda zsrc, sems, peer, more: x_all(zsrc))
    both(zs - 2, lambda zsrc, sems, peer, more: y_arrive(zsrc))
    both(zs - 1, lambda zsrc, sems, peer, more: y_arrive(zsrc))

    def finish(zsrc, carry):
        far = zsrc != z

        def sent(k):
            @pl.when(has_up & (zsrc <= z))
            def _():
                z_copy(zsrc, k, up_s, up_id).wait_send()

            @pl.when(has_dn & (zsrc >= z))
            def _():
                z_copy(zsrc, k, dn_s, dn_id).wait_send()

            if k != 1:
                x_copy(zsrc, k, x).wait_send()
                cx_copy(c, zsrc, k).wait_send()

            @pl.when(far)
            def _():
                cz_copy(c, zsrc, k).wait_send()

        def came(k):
            @pl.when(far)
            def _():
                cz_copy(1 - c, zsrc, k).wait_recv()

            if k != 1:
                cx_copy(1 - c, zsrc, k).wait_recv()

        for k in range(3):
            when_tail(c, k, lambda k=k: sent(k))
            when_tail(1 - c, k, lambda k=k: came(k))
        y_copy(zsrc, 0).wait_send()
        cy_copy(c, zsrc).wait_send()
        cy_copy(1 - c, zsrc).wait_recv()
        return carry

    lax.fori_loop(0, zs, finish, 0)
    a1.wait_send()
    for k in range(3):
        when_tail(c, k, lambda k=k: (a2(k).wait_send(), a2_fwd(c, k).wait_send(), None)[-1])
    for i in range(3):
        e_copy(i).wait_send()
    for store in stores:
        store.wait()


def solution(mesh):
    groups, shards = mesh.shape["grp"], mesh.shape["shard"]
    zs = shards // 2

    def per_device(layer_inner, layer_weights, layer_moment, embed_inner, embed_weights, embed_moment, basis):
        f32, bf16 = jnp.float32, jnp.bfloat16
        rows, width = layer_weights.shape
        rows_g, rows_e = embed_inner.shape[1], embed_weights.shape[0]
        rank = basis.shape[1]
        quarter = width // (4 * LANES) * LANES
        wide = -(-width // LANES) * LANES
        layer, emb = (rows, width), (rows_e, width)
        dma = pltpu.SemaphoreType.DMA
        any_ = pl.BlockSpec(memory_space=pl.ANY)
        new, mom, whole, enew, emom = pl.pallas_call(
            functools.partial(kernel, zs, groups, quarter),
            out_shape=(
                jax.ShapeDtypeStruct(layer, f32),
                jax.ShapeDtypeStruct(layer, f32),
                jax.ShapeDtypeStruct((shards, rows, wide), bf16),
                jax.ShapeDtypeStruct(emb, f32),
                jax.ShapeDtypeStruct(emb, f32),
            ),
            in_specs=[any_] * 7,
            out_specs=(any_,) * 5,
            scratch_shapes=[
                pltpu.VMEM(layer, f32), pltpu.VMEM(layer, f32), pltpu.VMEM(layer, f32), pltpu.VMEM(layer, f32),
                pltpu.VMEM((rows_g, width), f32), pltpu.VMEM(emb, f32), pltpu.VMEM(emb, f32),
                pltpu.VMEM((rank, width), f32),
                pltpu.VMEM((rows, wide), bf16), pltpu.VMEM((rows, wide), bf16), pltpu.VMEM((rows, wide), bf16),
                pltpu.VMEM(layer, f32), pltpu.VMEM(layer, f32),
                pltpu.VMEM((groups, rows_e, rank), f32), pltpu.VMEM((3, rows_e, rank), f32),
                pltpu.VMEM(emb, f32), pltpu.VMEM(emb, f32),
                dma((7,)), dma((5,)), dma, dma, dma((3,)), dma((3,)), dma((3,)), dma((3,)), dma((3,)), dma((3,)),
                dma((zs, 3)), dma((zs, 3)), dma((zs, 3)), dma((zs, 2)), dma((zs, 2)), dma((zs,)), dma((zs,)),
                dma((zs, 3)), dma((zs, 3)), dma((zs, 2)), dma((zs, 2)), dma((zs,)), dma((zs,)),
            ],
            compiler_params=pltpu.CompilerParams(
                collective_id=0, has_side_effects=True, vmem_limit_bytes=40 * 1024 * 1024
            ),
        )(layer_inner, layer_weights, layer_moment, embed_inner, embed_weights, embed_moment, basis.T)
        layer_copy = whole[:, :, :width].reshape(shards * rows, width)
        return new, mom, layer_copy, enew, emom

    in_specs = (
        P("grp", "shard", None),
        P("shard", None),
        P("shard", None),
        P("grp", "shard", None),
        P(("shard", "grp"), None),
        P(("shard", "grp"), None),
        P(),
    )
    out_specs = (
        P("shard", None),
        P("shard", None),
        P(),
        P(("shard", "grp"), None),
        P(("shard", "grp"), None),
    )
    return jax.shard_map(
        per_device, mesh=mesh, in_specs=in_specs, out_specs=out_specs, check_vma=False
    )
```

time: 157 us -> 66.9 us (0.43)
  waiting for transfers between devices: 112 us -> 0 us
  Pallas kernels: 0 us -> 47.8 us
  between operations: 14.8 us -> 0.66 us
  local copies, waits for them, and re-layouts: 6.17 us -> 18 us
  blocking collectives: 8.23 us -> 0 us
  matrix products: 7.27 us -> 0 us
  other arithmetic: 7.27 us -> 0 us
    all_gather x1 -> x0, waiting for transfers between devices: 69 us -> none  [per_device(): lax.all_gather(layer_new.astype(jnp.bfloat16), 'shard', axis=0, tiled=True)]
    pallas_call x0 -> x1, Pallas kernels: none -> 47.8 us  [per_device(): pl.pallas_call(functools.partial(kernel, zs, groups, quarter), out_shape=...]
    psum x1 -> x0, waiting for transfers between devices: 42.7 us -> none  [per_device(): average = lax.psum(own_diff, 'grp') / groups]
    unnamed x10 -> x19, local copies, waits for them, and re-layouts: 6.17 us -> 18 us
    unnamed x1 -> x0, blocking collectives: 8.23 us -> none
    dot_general x3 -> x0, matrix products: 7.27 us -> none  [the longest x1 3.2 us: per_device(): embed_step = jnp.dot(factors, basis.T, precision=lax.Precision.HIGHEST)]
    convert_element_type x1 -> x0, other arithmetic: 4.2 us -> none  [per_device(): layer_new.astype(jnp.bfloat16)]
    sub x1 -> x0, other arithmetic: 3.07 us -> none  [per_device(): own_diff = layer_weights - layer_inner[0]]
  transfers between devices with their start and end apart: 3 -> 0, of which waited for: 2 -> 0; matrix products, arithmetic and copies ran while one was open for 10% -> 0% of each run, Pallas kernels for 0% -> 0%
where the time goes in v1:
time: 66.9 us; the launch traced here: 66.5 us
  Pallas kernels  47.8 us (71%)
  local copies, waits for them, and re-layouts  18 us (27%)
    pallas_call x1, Pallas kernels, per_device(): pl.pallas_call(functools.partial(kernel, zs, groups, quarter), out_shape=...  47.8 us
    unnamed x19, local copies, waits for them, and re-layouts  18 us

profile of v1, /device:TPU:0, one launch (start us, length us, event | category | flops | bytes accessed | tf_op | source)
XLA Modules:
  0.0 66.5 jit_solution(17746562001281350784)
XLA Ops:
  0.6 0.0 copy-start
  0.6 1.7 %copy-done = f32[1,400,1600]{2,1,0:T(8,128)S(1)} copy-done((f32[1,400,1600]{2,1,0:T(8,128)S(1)}, f32[1,400,1600]{2,1,0:T(8,128)}, u32[]{:S(2)}) %copy-start) | copy-done | bytes 2560024
  2.4 0.0 copy-start.1
  2.4 1.3 %copy-done.1 = f32[1,200,1600]{2,1,0:T(8,128)S(1)} copy-done((f32[1,200,1600]{2,1,0:T(8,128)S(1)}, f32[1,200,1600]{2,1,0:T(8,128)}, u32[]{:S(2)}) %copy-start.1) | copy-done | bytes 1280024
  3.7 0.0 copy-start.2
  3.7 1.3 %copy-done.2 = f32[200,1600]{1,0:T(8,128)S(1)} copy-done((f32[200,1600]{1,0:T(8,128)S(1)}, f32[200,1600]{1,0:T(8,128)}, u32[]{:S(2)}) %copy-start.2) | copy-done | bytes 1280024
  5.0 0.0 copy-start.3
  5.0 1.3 %copy-done.3 = f32[200,1600]{1,0:T(8,128)S(1)} copy-done((f32[200,1600]{1,0:T(8,128)S(1)}, f32[200,1600]{1,0:T(8,128)}, u32[]{:S(2)}) %copy-start.3) | copy-done | bytes 1280024
  6.4 0.0 copy-start.4
  6.4 1.1 %copy-done.4 = f32[100,1600]{1,0:T(8,128)S(1)} copy-done((f32[100,1600]{1,0:T(8,128)S(1)}, f32[100,1600]{1,0:T(8,128)}, u32[]{:S(2)}) %copy-start.4) | copy-done | bytes 640024
  7.5 0.0 copy-start.5
  7.5 1.1 %copy-done.5 = f32[100,1600]{1,0:T(8,128)S(1)} copy-done((f32[100,1600]{1,0:T(8,128)S(1)}, f32[100,1600]{1,0:T(8,128)}, u32[]{:S(2)}) %copy-start.5) | copy-done | bytes 640024
  8.6 0.0 copy-start.6
  8.6 1.0 %copy-done.6 = f32[1600,64]{0,1:T(8,128)S(1)} copy-done((f32[1600,64]{0,1:T(8,128)S(1)}, f32[1600,64]{0,1:T(8,128)}, u32[]{:S(2)}) %copy-start.6) | copy-done | bytes 409624
  9.6 47.8 %shard_map.110 = (f32[200,1600]{1,0:T(8,128)S(1)}, f32[200,1600]{1,0:T(8,128)S(1)}, bf16[8,200,1664]{2,1,0:T(8,128)(2,1)}, f32[100,1600]{1,0:T(8,128)S(1)}, f32[100,1600]{1,0:T(8,128)S(1)}) custom-call(f32[1,200,1600]{2,1,0:T(8,128)S(1)} %copy-done.1, f32[200,1600]{1,0:T(8,128)S(1)} %copy-done.2, f32[200,1600]{1,0:T(8,128)S(1)} %copy-done.3, ...), custom_call_target="tpu_custom_call" | custom-call | tf_op jit(solution)/shard_map/pallas_call | solution.py:355
  57.4 1.1 %copy.17 = f32[200,1600]{1,0:T(8,128)} copy(f32[200,1600]{1,0:T(8,128)S(1)} %get-tuple-element.20) | data formatting | bytes 2560000
  58.5 1.1 %copy.18 = f32[200,1600]{1,0:T(8,128)} copy(f32[200,1600]{1,0:T(8,128)S(1)} %get-tuple-element.21) | data formatting | bytes 2560000
  59.5 5.3 %copy.19 = bf16[1600,1600]{1,0:T(8,128)(2,1)} copy(bf16[1600,1600]{1,0:T(8,128)(2,1)} %bitcast.4) | data formatting | bytes 10240000
  64.8 0.8 %copy.20 = f32[100,1600]{1,0:T(8,128)} copy(f32[100,1600]{1,0:T(8,128)S(1)} %get-tuple-element.23) | data formatting | bytes 1280000
  65.6 0.8 %copy.21 = f32[100,1600]{1,0:T(8,128)} copy(f32[100,1600]{1,0:T(8,128)S(1)} %get-tuple-element.24) | data formatting | bytes 1280000
Async XLA Ops:
  0.6 1.8 %copy-start = (f32[1,400,1600]{2,1,0:T(8,128)S(1)}, f32[1,400,1600]{2,1,0:T(8,128)}, u32[]{:S(2)}) copy-start(f32[1,400,1600]{2,1,0:T(8,128)} %einner_h.1) | copy-start | bytes 7680004
  2.4 1.3 %copy-start.1 = (f32[1,200,1600]{2,1,0:T(8,128)S(1)}, f32[1,200,1600]{2,1,0:T(8,128)}, u32[]{:S(2)}) copy-start(f32[1,200,1600]{2,1,0:T(8,128)} %inner_h.1) | copy-start | bytes 3840004
  3.7 1.3 %copy-start.2 = (f32[200,1600]{1,0:T(8,128)S(1)}, f32[200,1600]{1,0:T(8,128)}, u32[]{:S(2)}) copy-start(f32[200,1600]{1,0:T(8,128)} %w_h.1) | copy-start | bytes 3840004
  5.0 1.3 %copy-start.3 = (f32[200,1600]{1,0:T(8,128)S(1)}, f32[200,1600]{1,0:T(8,128)}, u32[]{:S(2)}) copy-start(f32[200,1600]{1,0:T(8,128)} %m_h.1) | copy-start | bytes 3840004
  6.4 1.1 %copy-start.4 = (f32[100,1600]{1,0:T(8,128)S(1)}, f32[100,1600]{1,0:T(8,128)}, u32[]{:S(2)}) copy-start(f32[100,1600]{1,0:T(8,128)} %ew_h.1) | copy-start | bytes 1920004
  7.5 1.1 %copy-start.5 = (f32[100,1600]{1,0:T(8,128)S(1)}, f32[100,1600]{1,0:T(8,128)}, u32[]{:S(2)}) copy-start(f32[100,1600]{1,0:T(8,128)} %em_h.1) | copy-start | bytes 1920004
  8.6 1.0 %copy-start.6 = (f32[1600,64]{0,1:T(8,128)S(1)}, f32[1600,64]{0,1:T(8,128)}, u32[]{:S(2)}) copy-start(f32[1600,64]{0,1:T(8,128)} %param.13) | copy-start | bytes 1228804

commit v2 on v1

--- a/solution.py
+++ b/solution.py
@@ -11,6 +11,7 @@
 momentum_coef = 0.9
 MESH = pl.DeviceIdType.MESH
 LANES = 128
+VMEM_LIMIT = 24 * 1024 * 1024
 SLOPE = 13.0
 SHIFT = 78.0
 
@@ -29,6 +30,11 @@
     code = code.astype(jnp.float32)
     size = (jnp.log(jnp.abs(code)) + SHIFT) * (1.0 / SLOPE)
     return jnp.where(code < 0, -size, size)
+
+
+def split(a):
+    high = a.astype(jnp.bfloat16)
+    return high, (a - high.astype(jnp.float32)).astype(jnp.bfloat16)
 
 
 def kernel(
@@ -82,13 +88,17 @@
             src_ref=src, dst_ref=dst, send_sem=ssem, recv_sem=rsem, device_id=peer, device_id_type=MESH
         )
 
-    a1 = remote(inner_h.at[0], sib, a1_s, a1_r, sib_id)
-    a1.start()
-    loads[0].wait()
-    a1.wait_recv()
-    code[:, :tail0] = encode(inner[:, :tail0] + sib[:, :tail0])
+    def a1(i, receiver):
+        if i == 1:
+            at = pl.ds(tail0, width - tail0)
+        else:
+            core = receiver if i == 0 else 1 - receiver
+            at = pl.ds(pl.multiple_of(core * 2 * quarter, LANES), 2 * quarter)
+        return remote(inner_h.at[0, :, at], sib.at[:, at], a1_s.at[i], a1_r.at[i], sib_id)
+
+    for i in range(3):
+        a1(i, 1 - c).start()
     code[:, tail0:] = jnp.zeros_like(code[:, tail0:])
-    code[:, tail0:width] = encode(inner[:, tail0:] + sib[:, tail0:])
 
     def cols(core, k):
         if k == 2:
@@ -113,14 +123,32 @@
         at = cols(core, k)
         return remote(rcode.at[:, at], rcode.at[:, at], a2f_s.at[k], a2f_r.at[k], sib_id)
 
-    for k in range(3):
-        when_tail(c, k, lambda k=k: a2(k).start())
+    def add_pair(at):
+        code[:, at] = encode(inner[:, at] + sib[:, at])
+
+    loads[0].wait()
+    a1(0, c).wait_recv()
+    for k in range(2):
+        add_pair(cols(c, 1 - k))
+        a2(k).start()
+    a1(1, c).wait_recv()
+    add_pair(pl.ds(tail0, width - tail0))
+    pl.when(c == 1)(lambda: a2(2).start())
 
     loads[1].wait()
     loads[2].wait()
     nt = (((1,), (1,)), ((), ()))
-    hi = lax.Precision.HIGHEST
-    inner_proj = lax.dot_general(einner[...], bt[...], nt, precision=hi, preferred_element_type=jnp.float32)
+    basis_parts = jnp.concatenate(split(bt[...]), axis=0)
+    rank = bt.shape[0]
+
+    def project(a):
+        total = 0.0
+        for part in split(a):
+            both_parts = lax.dot_general(part, basis_parts, nt, preferred_element_type=jnp.float32)
+            total = total + (both_parts[:, :rank] + both_parts[:, rank:])
+        return total
+
+    inner_proj = project(einner[...])
     for i in range(groups):
         proj[i] = inner_proj[i * rows_e : (i + 1) * rows_e]
     e_peers = (sib_id, y_id, diag_id)
@@ -130,6 +158,8 @@
 
     for i in range(3):
         e_copy(i).start()
+    a1(2, c).wait_recv()
+    add_pair(pl.ds(pl.multiple_of((1 - c) * 2 * quarter, LANES), 2 * quarter))
 
     loads[3].wait()
     loads[4].wait()
@@ -215,11 +245,16 @@
 
     loads[5].wait()
     loads[6].wait()
-    own_proj = lax.dot_general(ew[...], bt[...], nt, precision=hi, preferred_element_type=jnp.float32)
+    own_proj = project(ew[...])
     for i in range(3):
         e_copy(i).wait_recv()
     mean_proj = (proj[g] + precv[0] + precv[1] + precv[2]) * (1.0 / groups)
-    step = jnp.dot(own_proj - mean_proj, bt[...], precision=hi, preferred_element_type=jnp.float32)
+    high, low = split(own_proj - mean_proj)
+    step = jnp.dot(
+        jnp.concatenate([high, high, low, low], axis=1),
+        jnp.concatenate([basis_parts, basis_parts], axis=0),
+        preferred_element_type=jnp.float32,
+    )
     enew_v, emom_v = nesterov(ew[...], em[...], step)
     enew[...] = enew_v
     emom[...] = emom_v
@@ -329,7 +364,8 @@
         return carry
 
     lax.fori_loop(0, zs, finish, 0)
-    a1.wait_send()
+    for i in range(3):
+        a1(i, 1 - c).wait_send()
     for k in range(3):
         when_tail(c, k, lambda k=k: (a2(k).wait_send(), a2_fwd(c, k).wait_send(), None)[-1])
     for i in range(3):
@@ -351,6 +387,10 @@
         wide = -(-width // LANES) * LANES
         layer, emb = (rows, width), (rows_e, width)
         dma = pltpu.SemaphoreType.DMA
+        operands = [
+            pltpu.with_memory_space_constraint(a, pltpu.HBM)
+            for a in (layer_inner, layer_weights, layer_moment, embed_inner, embed_weights, embed_moment, basis.T)
+        ]
         any_ = pl.BlockSpec(memory_space=pl.ANY)
         new, mom, whole, enew, emom = pl.pallas_call(
             functools.partial(kernel, zs, groups, quarter),
@@ -361,7 +401,7 @@
                 jax.ShapeDtypeStruct(emb, f32),
                 jax.ShapeDtypeStruct(emb, f32),
             ),
-            in_specs=[any_] * 7,
+            in_specs=[pl.BlockSpec(memory_space=pltpu.HBM)] * 7,
             out_specs=(any_,) * 5,
             scratch_shapes=[
                 pltpu.VMEM(layer, f32), pltpu.VMEM(layer, f32), pltpu.VMEM(layer, f32), pltpu.VMEM(layer, f32),
@@ -371,14 +411,14 @@
                 pltpu.VMEM(layer, f32), pltpu.VMEM(layer, f32),
                 pltpu.VMEM((groups, rows_e, rank), f32), pltpu.VMEM((3, rows_e, rank), f32),
                 pltpu.VMEM(emb, f32), pltpu.VMEM(emb, f32),
-                dma((7,)), dma((5,)), dma, dma, dma((3,)), dma((3,)), dma((3,)), dma((3,)), dma((3,)), dma((3,)),
+                dma((7,)), dma((5,)), dma((3,)), dma((3,)), dma((3,)), dma((3,)), dma((3,)), dma((3,)), dma((3,)), dma((3,)),
                 dma((zs, 3)), dma((zs, 3)), dma((zs, 3)), dma((zs, 2)), dma((zs, 2)), dma((zs,)), dma((zs,)),
                 dma((zs, 3)), dma((zs, 3)), dma((zs, 2)), dma((zs, 2)), dma((zs,)), dma((zs,)),
             ],
             compiler_params=pltpu.CompilerParams(
-                collective_id=0, has_side_effects=True, vmem_limit_bytes=40 * 1024 * 1024
+                collective_id=0, has_side_effects=True, vmem_limit_bytes=VMEM_LIMIT
             ),
-        )(layer_inner, layer_weights, layer_moment, embed_inner, embed_weights, embed_moment, basis.T)
+        )(*operands)
         layer_copy = whole[:, :, :width].reshape(shards * rows, width)
         return new, mom, layer_copy, enew, emom
 

time: 66.9 us -> 51.2 us (0.77)
  local copies, waits for them, and re-layouts: 18 us -> 6.21 us
  Pallas kernels: 47.8 us -> 44.2 us
    unnamed x19 -> x5, local copies, waits for them, and re-layouts: 18 us -> 6.21 us
    pallas_call x1, Pallas kernels: 47.8 us -> 44.2 us  [per_device(): pl.pallas_call(functools.partial(kernel, zs, groups, quarter), out_shape=...]
where the time goes in v2:
time: 51.2 us; the launch traced here: 51 us
  Pallas kernels  44.2 us (86%)
  local copies, waits for them, and re-layouts  6.21 us (12%)
  between operations  0.64 us (1%)
    pallas_call x1, Pallas kernels, per_device(): pl.pallas_call(functools.partial(kernel, zs, groups, quarter), out_shape=...  44.2 us
    unnamed x5, local copies, waits for them, and re-layouts  6.21 us

profile of v2, /device:TPU:0, one launch (start us, length us, event | category | flops | bytes accessed | tf_op | source)
XLA Modules:
  0.0 51.0 jit_solution(512583419587746382)
XLA Ops:
  0.6 44.2 %shard_map.110 = (f32[200,1600]{1,0:T(8,128)S(1)}, f32[200,1600]{1,0:T(8,128)S(1)}, bf16[8,200,1664]{2,1,0:T(8,128)(2,1)S(1)}, f32[100,1600]{1,0:T(8,128)S(1)}, f32[100,1600]{1,0:T(8,128)S(1)}) custom-call(f32[1,200,1600]{2,1,0:T(8,128)} %inner_h.1, f32[200,1600]{1,0:T(8,128)} %w_h.1, f32[200,1600]{1,0:T(8,128)} %m_h.1, f32[1,400,1600]{2,1,0:T(8,128)} %einner_h.1, ...), custom_call_target="tpu_custom_call" | custom-call | tf_op jit(solution)/shard_map/pallas_call | solution.py:395
  44.8 1.1 %copy.17 = f32[200,1600]{1,0:T(8,128)} copy(f32[200,1600]{1,0:T(8,128)S(1)} %get-tuple-element.20) | data formatting | bytes 2560000
  45.9 1.1 %copy.18 = f32[200,1600]{1,0:T(8,128)} copy(f32[200,1600]{1,0:T(8,128)S(1)} %get-tuple-element.21) | data formatting | bytes 2560000
  46.9 2.4 %copy.19 = bf16[1600,1600]{1,0:T(8,128)(2,1)} copy(bf16[1600,1600]{1,0:T(8,128)(2,1)S(1)} %bitcast.3) | data formatting | bytes 10240000
  49.3 0.8 %copy.20 = f32[100,1600]{1,0:T(8,128)} copy(f32[100,1600]{1,0:T(8,128)S(1)} %get-tuple-element.23) | data formatting | bytes 1280000
  50.2 0.8 %copy.21 = f32[100,1600]{1,0:T(8,128)} copy(f32[100,1600]{1,0:T(8,128)S(1)} %get-tuple-element.24) | data formatting | bytes 1280000

commit v3 on v2

--- a/solution.py
+++ b/solution.py
@@ -372,6 +372,16 @@
         e_copy(i).wait_send()
     for store in stores:
         store.wait()
+
+
+def store_all(*refs):
+    sems = refs[-1]
+    count = len(refs) // 2
+    copies = [pltpu.make_async_copy(refs[i], refs[count + i], sems.at[i]) for i in range(count)]
+    for copy in copies:
+        copy.start()
+    for copy in copies:
+        copy.wait()
 
 
 def solution(mesh):
@@ -419,6 +429,14 @@
                 collective_id=0, has_side_effects=True, vmem_limit_bytes=VMEM_LIMIT
             ),
         )(*operands)
+        new, mom, enew, emom = pl.pallas_call(
+            store_all,
+            out_shape=[jax.ShapeDtypeStruct(shape, f32) for shape in (layer, layer, emb, emb)],
+            in_specs=[any_] * 4,
+            out_specs=[any_] * 4,
+            scratch_shapes=[dma((4,))],
+            compiler_params=pltpu.CompilerParams(vmem_limit_bytes=1024 * 1024),
+        )(new, mom, enew, emom)
         layer_copy = whole[:, :, :width].reshape(shards * rows, width)
         return new, mom, layer_copy, enew, emom
 

time: 51.2 us -> 49.3 us (0.963)
  local copies, waits for them, and re-layouts: 6.21 us -> 2.39 us
  Pallas kernels: 44.2 us -> 46.2 us
    unnamed x5 -> x1, local copies, waits for them, and re-layouts: 6.21 us -> 2.39 us
    pallas_call x0 -> x1, Pallas kernels: none -> 1.99 us  [per_device(): pl.pallas_call(store_all, out_shape=[jax.ShapeDtypeStruct(shape, f32) for...]
where the time goes in v3:
time: 49.3 us; the launch traced here: 49.2 us
  Pallas kernels  46.2 us (94%)
  local copies, waits for them, and re-layouts  2.39 us (5%)
  between operations  0.65 us (1%)
    pallas_call x1, Pallas kernels, per_device(): pl.pallas_call(functools.partial(kernel, zs, groups, quarter), out_shape=...  44.2 us
    unnamed x1, local copies, waits for them, and re-layouts  2.39 us
    pallas_call x1, Pallas kernels, per_device(): pl.pallas_call(store_all, out_shape=[jax.ShapeDtypeStruct(shape, f32) for...  1.99 us

profile of v3, /device:TPU:0, one launch (start us, length us, event | category | flops | bytes accessed | tf_op | source)
XLA Modules:
  0.0 49.2 jit_solution(17200655708480439263)
XLA Ops:
  0.6 44.2 %shard_map.110 = (f32[200,1600]{1,0:T(8,128)S(1)}, f32[200,1600]{1,0:T(8,128)S(1)}, bf16[8,200,1664]{2,1,0:T(8,128)(2,1)S(1)}, f32[100,1600]{1,0:T(8,128)S(1)}, f32[100,1600]{1,0:T(8,128)S(1)}) custom-call(f32[1,200,1600]{2,1,0:T(8,128)} %inner_h.1, f32[200,1600]{1,0:T(8,128)} %w_h.1, f32[200,1600]{1,0:T(8,128)} %m_h.1, f32[1,400,1600]{2,1,0:T(8,128)} %einner_h.1, ...), custom_call_target="tpu_custom_call" | custom-call | tf_op jit(solution)/shard_map/pallas_call | solution.py:405
  44.8 2.0 %shard_map.111 = (f32[200,1600]{1,0:T(8,128)}, f32[200,1600]{1,0:T(8,128)}, f32[100,1600]{1,0:T(8,128)}, f32[100,1600]{1,0:T(8,128)}) custom-call(f32[200,1600]{1,0:T(8,128)S(1)} %get-tuple-element.14.refs_0_, f32[200,1600]{1,0:T(8,128)S(1)} %get-tuple-element.15.refs_1_, f32[100,1600]{1,0:T(8,128)S(1)} %get-tuple-element.16.refs_2_, ...), custom_call_target="tpu_custom_call" | custom-call | tf_op jit(solution)/shard_map/pallas_call | solution.py:432
  46.8 2.4 %copy.13 = bf16[1600,1600]{1,0:T(8,128)(2,1)} copy(bf16[1600,1600]{1,0:T(8,128)(2,1)S(1)} %bitcast.3) | data formatting | bytes 10240000
